TPU v7x, 32 devices: a whole 2x2x4 slice. The times are simulated.
32 devices in a mesh: fsdp: 4 (over x, core), owner: 8 (over z, y).
Axes of the slice: x: 2, y: 2, z: 4, core: 2. Of those that a mesh axis runs over, the one named last changes fastest.
Arguments:
- grads: bfloat16 [16, 2560, 5120], P('owner', 'fsdp'), may hold values from -6 to 6
- assign: int32 [160, 1], replicated, may hold values from 0 to 7; in each aligned block of 20 rows (0 to 19, 20 to 39, ...) at most 4 rows name the same one
- bases: bfloat16 [8, 32, 512, 512], P('owner', None, 'fsdp'), may hold values from -0.25 to 0.25
- eigvals: bfloat16 [8, 32, 512], P('owner'), may hold values from 0.099609375 to 10
Outputs:
- update: bfloat16 [16, 2560, 5120], P('owner', 'fsdp')
Inputs may be any that keep to these rules, and one draw needn't show every extreme that they name: `assign`: within each aligned block of 20 units (the matrices of one index of owner) no owner is named more than 4 times; in some block one owner is named exactly 4 times.
All inputs are finite; a program needn't handle non-finite values.
Results may differ from a plain program's by a relative error of at most 0.0043.
Values may be sent and summed in bfloat16 or wider, within the bound.
A program may use at most 128 MiB of HBM per device.

v0:
```python
import jax
import jax.numpy as jnp
from jax import lax
from jax.sharding import PartitionSpec as P

BLK = 512


DAMPING = 0.1


def rotate(panel_block, basis_block, eigen_vals):
    turned = jnp.einsum(
        "srk,skc->src", panel_block, basis_block, preferred_element_type=jnp.float32
    )
    scaled = (turned / (eigen_vals.astype(jnp.float32)[:, None, :] + DAMPING)).astype(jnp.bfloat16)
    return jnp.einsum(
        "srk,sck->src", scaled, basis_block, preferred_element_type=jnp.float32
    ).astype(jnp.bfloat16)


def per_device(grads, assign, bases, eigvals):
    owner_count = lax.axis_size("owner")
    owner_here = lax.axis_index("owner")
    matrices, row_count, col_count = grads.shape
    block_count = col_count // BLK
    unit_count = matrices * block_count
    slot_count = bases.shape[1]
    per_peer = slot_count // owner_count
    owner_table = assign[:, 0].reshape(owner_count, unit_count)
    owner_ids = jnp.arange(owner_count, dtype=jnp.int32)
    owner_hits = (owner_table[:, :, None] == owner_ids[None, None, :]).astype(jnp.int32)
    slot_ranks = jnp.sum((jnp.cumsum(owner_hits, axis=1) - 1) * owner_hits, axis=2)
    my_owners = lax.dynamic_index_in_dim(owner_table, owner_here, 0, keepdims=False)
    my_rank = lax.dynamic_index_in_dim(slot_ranks, owner_here, 0, keepdims=False)
    my_slots = my_owners * per_peer + my_rank
    panels = (
        grads.reshape(matrices, row_count, block_count, BLK)
        .transpose(0, 2, 1, 3)
        .reshape(unit_count, row_count, BLK)
    )
    base_local = bases[0]
    eigen_local = eigvals[0]
    moved_bases, moved_eigen = (
        lax.all_to_all(base_local, "owner", split_axis=0, concat_axis=0, tiled=True),
        lax.all_to_all(eigen_local, "owner", split_axis=0, concat_axis=0, tiled=True),
    )
    full_bases = lax.all_gather(moved_bases, "fsdp", axis=1, tiled=True)
    finished = rotate(panels, full_bases[my_slots], moved_eigen[my_slots])
    return (
        finished.reshape(matrices, block_count, row_count, BLK)
        .transpose(0, 2, 1, 3)
        .reshape(matrices, row_count, col_count)
    )


def solution(mesh):
    in_specs = (
        P("owner", "fsdp", None),
        P(),
        P("owner", None, "fsdp", None),
        P("owner", None, None),
    )
    out_specs = P("owner", "fsdp", None)
    return jax.shard_map(
        per_device, mesh=mesh, in_specs=in_specs, out_specs=out_specs, check_vma=False
    )
```

profile of v0, /device:TPU:0, one launch (start us, length us, event | category | flops | bytes accessed | tf_op | source)
XLA Modules:
  0.0 271.2 jit_solution(232667497581358695)
XLA Ops:
  6.5 0.0 all-gather.2.cloned.1.call-start
  6.5 100.6 %all_to_all.17 = bf16[32,128,512]{2,1,0:T(8,128)(2,1)} all-to-all(bf16[32,128,512]{2,1,0:T(8,128)(2,1)} %bitcast.22), channel_id=1, replica_groups=mesh['fsdp'=4,'owner'=8] {'owner'}, dimensions={0} | all-to-all | bytes 8388608 | tf_op jit(solution)/shard_map/all_to_all | solution.py:45
  107.1 0.0 all-gather.2.cloned.1.call-update
  107.1 1.4 all_to_all.12
  108.5 3.6 %all-to-all-start.1 = ((bf16[8,4,512]{2,1,0:T(4,128)(2,1)}), bf16[8,4,512]{2,1,0:T(4,128)(2,1)S(1)}, u32[]{:S(2)}, u32[]{:S(2)}) async-start(bf16[8,4,512]{2,1,0:T(4,128)(2,1)} %all_to_all.12), calls=%async_computation.1 | async-start | bytes 65536 | tf_op jit(solution)/shard_map/all_to_all | solution.py:46
  112.1 0.5 broadcast.64
  112.6 1.4 reduce.5
  114.0 0.1 reshape_squeeze.3
  114.0 0.1 copy.15
  114.1 18.7 %copy.17 = bf16[2,640,5120]{1,2,0:T(8,128)(2,1)} copy(bf16[2,640,5120]{2,1,0:T(8,128)(2,1)} %param.4) | data formatting | bytes 26214400 | tf_op args[0]
  132.9 0.5 fusion.9
  133.4 0.2 add_reduce_fusion
  133.6 0.0 all-to-all-done.1
  133.6 0.6 gather_fusion.1
  134.2 78.0 %all-gather.2.cloned.1.call-done = bf16[32,512,512]{2,1,0:T(8,128)(2,1)} async-done(((bf16[32,128,512]{2,1,0:T(8,128)(2,1)}), bf16[32,512,512]{2,1,0:T(8,128)(2,1)}) %all-gather.2.cloned.1.call-update) | async-done | bytes 16777232 | tf_op jit(solution)/shard_map/all_gather | solution.py:48
  212.2 11.3 %gather_fusion = bf16[20,512,512]{2,1,0:T(8,128)(2,1)} fusion(bf16[32,512,512]{2,1,0:T(8,128)(2,1)} %all-gather.2.cloned.1.call-done, s32[1024]{0:T(1024)S(1)} %pad_clamp_fusion), kind=kCustom, calls=%fused_computation | custom fusion | bytes 20971600 | tf_op jit(solution)/shard_map/gather | solution.py:49
  223.5 23.2 %fusion.2 = bf16[20,640,512]{1,2,0:T(8,128)(2,1)} fusion(bf16[20,512,512]{2,1,0:T(8,128)(2,1)} %gather_fusion, f32[20,512]{1,0:T(8,128)S(1)} %convert_add_fusion, bf16[20,640,512]{1,2,0:T(8,128)(2,1)} %bitcast.20), kind=kOutput, calls=%fused_computation.5 | convolution fusion | flops 13441433600 | bytes 36741120 | tf_op jit(solution)/shard_map/srk,sck->src/dot_general | solution.py:17
  246.7 17.6 %copy.20 = bf16[2,640,5120]{2,1,0:T(8,128)(2,1)} copy(bf16[2,640,5120]{1,2,0:T(8,128)(2,1)} %bitcast.21) | data formatting | bytes 26214400 | tf_op jit(solution)/shard_map/reshape | solution.py:53
  (4 shorter events, 0.0 us)
Async XLA Ops:
  6.5 205.7 %all-gather.2.cloned.1.call-start = ((), (), s32[]{:S(2)}) async-start(), calls=%async_computation.2 | async-start | bytes 20971520 | tf_op jit(solution)/shard_map/all_gather | solution.py:48
  108.5 25.1 %all-to-all-start.1 = ((bf16[8,4,512]{2,1,0:T(4,128)(2,1)}), bf16[8,4,512]{2,1,0:T(4,128)(2,1)S(1)}, u32[]{:S(2)}, u32[]{:S(2)}) async-start(bf16[8,4,512]{2,1,0:T(4,128)(2,1)} %all_to_all.12), calls=%async_computation.1 | async-start | bytes 65536 | tf_op jit(solution)/shard_map/all_to_all | solution.py:46
Sparse Core Ops, SparseCore 0:
  107.2 104.9 all-gather.1
where the time goes:
time: 272 us; the launch traced here: 271 us
  blocking collectives  101 us (37%)
  waiting for transfers between devices  78 us (29%)
  local copies, waits for them, and re-layouts  50.3 us (18%)
  matrix products  23.2 us (9%)
  between operations  13.4 us (5%)
  starting transfers between devices  3.59 us (1%)
    all_to_all x1, blocking collectives, per_device(): lax.all_to_all(base_local, 'owner', split_axis=0, concat_axis=0, tiled=True)  101 us
    all_gather x1, waiting for transfers between devices, per_device(): full_bases = lax.all_gather(moved_bases, 'fsdp', axis=1, tiled=True)  78 us
    dot_general x1, matrix products, rotate(): jnp.einsum('srk,sck->src', scaled, basis_block, preferred_element_type=jn...  23.2 us
    unnamed x2, local copies, waits for them, and re-layouts  19.3 us
    reshape x1, local copies, waits for them, and re-layouts, per_device(): return finished.reshape(matrices, block_count, row_count, BLK).transpose(...  17.6 us
    gather x2, local copies, waits for them, and re-layouts, per_device(): finished = rotate(panels, full_bases[my_slots], moved_eigen[my_slots])  11.9 us
  transfers between devices with their start and end apart: 2, of which 1 were waited for; matrix products, arithmetic and copies ran while one was open for 8% of the time, Pallas kernels for 0%

commit v1 on v0

v1 whole, which is shorter than its diff:
```python
import functools
import jax
import jax.numpy as jnp
from jax import lax
from jax.experimental import pallas as pl
from jax.experimental.pallas import tpu as pltpu
from jax.sharding import PartitionSpec as P

BLK = 512
DAMPING = 0.1


def rotate_kernel(first, kinds, unit_ref, rank_ref, owner_ref, *refs):
    panel_ref, inverse_ref = refs[0], refs[1]
    basis_refs, out_ref = refs[2 : 2 + kinds], refs[-1]
    rank = rank_ref[first + pl.program_id(0)]
    for kind in range(kinds):

        @pl.when(rank == kind)
        def _():
            basis = basis_refs[kind][0]
            turned = jnp.dot(panel_ref[0], basis, preferred_element_type=jnp.float32)
            scaled = (turned * inverse_ref[0]).astype(jnp.bfloat16)
            out_ref[0] = lax.dot_general(
                scaled, basis, (((1,), (1,)), ((), ())), preferred_element_type=jnp.float32
            ).astype(jnp.bfloat16)


def rotate(first, count, blocks, last_packed, scalars, grads, inverse, bases, so_far):
    row_count = grads.shape[1]
    kinds = len(bases)

    def panel_map(i, unit, rank, owner):
        u = unit[first + i]
        return u // blocks, 0, u % blocks

    def inverse_map(i, unit, rank, owner):
        return first + i, 0, 0

    def basis_map(kind, i, unit, rank, owner):
        place = i if last_packed and kind == kinds - 1 else owner[first + i]
        return jnp.where(rank[first + i] == kind, place, 0), 0, 0

    in_specs = [
        pl.BlockSpec((1, row_count, BLK), panel_map),
        pl.BlockSpec((1, 1, BLK), inverse_map),
    ] + [pl.BlockSpec((1, BLK, BLK), functools.partial(basis_map, kind)) for kind in range(kinds)]
    operands = [grads, inverse, *bases]
    aliases = {}
    if so_far is not None:
        in_specs.append(pl.BlockSpec(memory_space=pl.ANY))
        aliases = {len(scalars) + len(operands): 0}
        operands.append(so_far)
    return pl.pallas_call(
        functools.partial(rotate_kernel, first, kinds),
        grid_spec=pltpu.PrefetchScalarGridSpec(
            num_scalar_prefetch=len(scalars),
            grid=(count,),
            in_specs=in_specs,
            out_specs=pl.BlockSpec((1, row_count, BLK), panel_map),
        ),
        out_shape=jax.ShapeDtypeStruct(grads.shape, grads.dtype),
        input_output_aliases=aliases,
        compiler_params=pltpu.CompilerParams(vmem_limit_bytes=60 * 1024 * 1024),
        cost_estimate=pl.CostEstimate(
            flops=count * 4 * row_count * BLK * BLK,
            bytes_accessed=count * (4 * row_count * BLK + 2 * BLK * BLK),
            transcendentals=0,
        ),
        name="rotate",
    )(*scalars, *operands)


def per_device(grads, assign, bases, eigvals):
    owner_count = lax.axis_size("owner")
    owner_here = lax.axis_index("owner")
    matrices, row_count, col_count = grads.shape
    block_count = col_count // BLK
    unit_count = matrices * block_count
    slot_count = bases.shape[1]
    per_peer = slot_count // owner_count

    all_eigen = lax.all_gather(eigvals[0], "owner", axis=0, tiled=False)

    units = jnp.arange(unit_count, dtype=jnp.int32)
    owners = lax.dynamic_slice_in_dim(assign[:, 0], owner_here * unit_count, unit_count)
    earlier = units[None, :] < units[:, None]
    ranks = jnp.sum((owners[None, :] == owners[:, None]) & earlier, axis=1, dtype=jnp.int32)
    before = (ranks[None, :] < ranks[:, None]) | ((ranks[None, :] == ranks[:, None]) & earlier)
    places = jnp.sum(before, axis=1, dtype=jnp.int32)
    code = (ranks * owner_count + owners) * unit_count + units
    code = jnp.sum(jnp.where(places[None, :] == units[:, None], code[None, :], 0), axis=1, dtype=jnp.int32)
    unit_at = code % unit_count
    owner_at = code // unit_count % owner_count
    rank_at = code // (unit_count * owner_count)
    scalars = (unit_at, rank_at, owner_at)

    tail = unit_count // per_peer
    head = unit_count - tail
    local = bases[0].reshape((owner_count, per_peer) + bases.shape[2:])
    full = []
    for rank in range(per_peer):
        moved = lax.all_to_all(local[:, rank], "owner", split_axis=0, concat_axis=0, tiled=True)
        if rank == per_peer - 1:
            moved = moved[owner_at[head:]]
        full.append(lax.all_gather(moved, "fsdp", axis=1, tiled=True))

    eigen = all_eigen[owner_at, owner_here * per_peer + rank_at]
    inverse = (1.0 / (eigen.astype(jnp.float32) + DAMPING))[:, None, :]
    out = rotate(0, head, block_count, False, scalars, grads, inverse, full[:-1], None)
    return rotate(head, tail, block_count, True, scalars, grads, inverse, full, out)


def solution(mesh):
    in_specs = (
        P("owner", "fsdp", None),
        P(),
        P("owner", None, "fsdp", None),
        P("owner", None, None),
    )
    out_specs = P("owner", "fsdp", None)
    return jax.shard_map(
        per_device, mesh=mesh, in_specs=in_specs, out_specs=out_specs, check_vma=False
    )
```

time: 272 us -> 201 us (0.74)
  waiting for transfers between devices: 78 us -> 24.2 us
  local copies, waits for them, and re-layouts: 50.3 us -> 6.55 us
  Pallas kernels: 0 us -> 30 us
  matrix products: 23.2 us -> 0 us
  blocking collectives: 101 us -> 121 us
    all_gather x1 -> x4, waiting for transfers between devices: 78 us -> 0.01 us  [per_device(): full.append(lax.all_gather(moved, 'fsdp', axis=1, tiled=True))]
    all_gather x0 -> x1, blocking collectives: none -> 30.7 us  [per_device(): all_eigen = lax.all_gather(eigvals[0], 'owner', axis=0, tiled=False)]
    pallas_call x0 -> x2, Pallas kernels: none -> 30 us  [rotate(): pl.pallas_call(functools.partial(rotate_kernel, first, kinds), grid_spec=...]
    all_to_all x1, waiting for transfers between devices: 0.01 us -> 24.1 us  [per_device(): lax.all_to_all(local[:, rank], 'owner', split_axis=0, concat_axis=0, tile...]
    dot_general x1 -> x0, matrix products: 23.2 us -> none  [rotate(): jnp.einsum('srk,sck->src', scaled, basis_block, preferred_element_type=jn...]
    unnamed x2 -> x6, local copies, waits for them, and re-layouts: 19.3 us -> 0.01 us
    reshape x1 -> x0, local copies, waits for them, and re-layouts: 17.6 us -> none  [per_device(): return finished.reshape(matrices, block_count, row_count, BLK).transpose(...]
    all_to_all x1 -> x3, blocking collectives: 101 us -> 90.7 us  [per_device(): lax.all_to_all(local[:, rank], 'owner', split_axis=0, concat_axis=0, tile...]
  transfers between devices with their start and end apart: 2 -> 5, of which waited for: 1 -> 1; matrix products, arithmetic and copies ran while one was open for 8% -> 2% of each run, Pallas kernels for 0% -> 11%
where the time goes in v1:
time: 201 us; the launch traced here: 200 us
  blocking collectives  121 us (60%)
  Pallas kernels  30 us (15%)
  waiting for transfers between devices  24.2 us (12%)
  between operations  13.2 us (7%)
  local copies, waits for them, and re-layouts  6.55 us (3%)
  starting transfers between devices  3.7 us (2%)
    all_to_all x3, blocking collectives, per_device(): lax.all_to_all(local[:, rank], 'owner', split_axis=0, concat_axis=0, tile...  90.7 us
    all_gather x1, blocking collectives, per_device(): all_eigen = lax.all_gather(eigvals[0], 'owner', axis=0, tiled=False)  30.7 us
    pallas_call x2, Pallas kernels, rotate(): pl.pallas_call(functools.partial(rotate_kernel, first, kinds), grid_spec=...  30 us
    all_to_all x1, waiting for transfers between devices, per_device(): lax.all_to_all(local[:, rank], 'owner', split_axis=0, concat_axis=0, tile...  24.1 us
  transfers between devices with their start and end apart: 5, of which 1 were waited for; matrix products, arithmetic and copies ran while one was open for 2% of the time, Pallas kernels for 11%

profile of v1, /device:TPU:0, one launch (start us, length us, event | category | flops | bytes accessed | tf_op | source)
XLA Modules:
  0.0 200.3 jit_solution(6648629621043934517)
XLA Ops:
  6.5 0.0 all-gather.8.cloned.1.call-start
  6.5 3.5 %slice_bitcast_fusion = (bf16[8,128,512]{2,1,0:T(8,128)(2,1)}, bf16[8,128,512]{2,1,0:T(8,128)(2,1)S(1)}, bf16[8,128,512]{2,1,0:T(8,128)(2,1)S(1)}, bf16[8,128,512]{2,1,0:T(8,128)(2,1)S(1)}) fusion(bf16[8,4,128,512]{3,2,1,0:T(8,128)(2,1)} %bitcast.49), kind=kLoop, calls=%fused_computation.2 | loop fusion | bytes 8388608 | tf_op jit(solution)/shard_map/squeeze | solution.py:103
  10.1 32.9 %all_to_all.20 = bf16[8,128,512]{2,1,0:T(8,128)(2,1)} all-to-all(bf16[8,128,512]{2,1,0:T(8,128)(2,1)S(1)} %get-tuple-element.6), channel_id=1, replica_groups=mesh['fsdp'=4,'owner'=8] {'owner'}, dimensions={0} | all-to-all | bytes 2097152 | tf_op jit(solution)/shard_map/all_to_all | solution.py:103
  43.0 0.0 all-gather.8.cloned.1.call-update
  43.0 0.0 all-gather.6.cloned.1.call-start
  43.1 0.0 copy-start.2
  43.1 29.0 %all_to_all.21 = bf16[8,128,512]{2,1,0:T(8,128)(2,1)} all-to-all(bf16[8,128,512]{2,1,0:T(8,128)(2,1)S(1)} %get-tuple-element.7), channel_id=1, replica_groups=mesh['fsdp'=4,'owner'=8] {'owner'}, dimensions={0} | all-to-all | bytes 2097152 | tf_op jit(solution)/shard_map/all_to_all | solution.py:103
  72.1 0.0 copy-start
  72.1 0.0 all-gather.6.cloned.1.call-update
  72.1 0.0 all-gather.10.cloned.1.call-start
  72.1 28.8 %all_to_all.22 = bf16[8,128,512]{2,1,0:T(8,128)(2,1)} all-to-all(bf16[8,128,512]{2,1,0:T(8,128)(2,1)S(1)} %get-tuple-element.8), channel_id=1, replica_groups=mesh['fsdp'=4,'owner'=8] {'owner'}, dimensions={0} | all-to-all | bytes 2097152 | tf_op jit(solution)/shard_map/all_to_all | solution.py:103
  100.9 0.0 all-gather.10.cloned.1.call-update
  100.9 3.6 %all-to-all-start.3 = ((bf16[8,128,512]{2,1,0:T(8,128)(2,1)}), bf16[8,128,512]{2,1,0:T(8,128)(2,1)S(1)}, u32[]{:S(2)}, u32[]{:S(2)}) async-start(bf16[8,128,512]{2,1,0:T(8,128)(2,1)} %get-tuple-element.5), calls=%async_computation.3 | async-start | bytes 2097152 | tf_op jit(solution)/shard_map/all_to_all | solution.py:103
  104.5 0.0 all-gather.12.cloned.1.call-start
  104.6 0.0 copy-done.2
  104.6 0.1 dynamic-slice_bitcast_fusion
  104.7 0.2 convert_reduce_fusion.1
  104.8 0.2 convert_reduce_fusion
  105.0 0.1 iota_add_fusion
  105.1 0.1 select_reduce_fusion
  105.2 0.6 and_select_fusion.1
  105.8 0.1 compare_select_fusion
  105.9 24.1 %all-to-all-done.3 = bf16[8,128,512]{2,1,0:T(8,128)(2,1)S(1)} async-done(((bf16[8,128,512]{2,1,0:T(8,128)(2,1)}), bf16[8,128,512]{2,1,0:T(8,128)(2,1)S(1)}, u32[]{:S(2)}, u32[]{:S(2)}) %all-to-all-start.3) | async-done | bytes 1048608 | tf_op jit(solution)/shard_map/all_to_all | solution.py:103
  130.0 1.5 gather_fusion.1
  131.5 0.0 all-gather.12.cloned.1.call-update
  131.5 0.0 copy-done
  131.5 30.7 %all_gather.15 = bf16[8,32,512]{2,1,0:T(8,128)(2,1)S(1)} all-gather(bf16[1,32,512]{2,1,0:T(8,128)(2,1)S(1)} %copy-done), channel_id=1, replica_groups=mesh['fsdp'=4,'owner'=8] {'owner'}, dimensions={0}, use_global_device_ids=true | all-gather | bytes 294912 | tf_op jit(solution)/shard_map/all_gather | solution.py:83
  162.3 0.8 gather_fusion
  163.1 0.6 div.52.refs_1_
  163.7 0.0 copy-done.1
  163.8 21.1 %rotate.2.refs_6_ = bf16[2,640,5120]{2,1,0:T(8,128)(2,1)} custom-call(s32[20]{0:T(128)} %get-tuple-element.11.unit_ref, s32[20]{0:T(128)} %get-tuple-element.10.rank_ref, s32[20]{0:T(128)} %copy-done.1, bf16[2,640,5120]{2,1,0:T(8,128)(2,1)} %refs_0_.3, f32[20,1,512]{2,1,0:T(1,128)} %div.52.refs_1_, ...), custom_call_target="tpu_custom_call" | custom-call | flops 10066329600 | bytes 27525120 | tf_op jit(solution)/shard_map/rotate/pallas_call | solution.py:54
  184.8 9.0 %rotate.3 = bf16[2,640,5120]{2,1,0:T(8,128)(2,1)} custom-call(s32[20]{0:T(128)} %get-tuple-element.11.unit_ref, s32[20]{0:T(128)} %get-tuple-element.10.rank_ref, s32[20]{0:T(128)} %copy-done.1, bf16[2,640,5120]{2,1,0:T(8,128)(2,1)} %refs_0_.3, f32[20,1,512]{2,1,0:T(1,128)} %div.52.refs_1_, ...), custom_call_target="tpu_custom_call", output_to_operand_aliasing={{}: (9, {})} | custom-call | flops 3355443200 | bytes 9175040 | tf_op jit(solution)/shard_map/rotate/pallas_call | solution.py:54
  (8 shorter events, 0.1 us)
Async XLA Ops:
  6.5 157.2 %all-gather.8.cloned.1.call-start = ((), (), s32[]{:S(2)}) async-start(), calls=%async_computation.5 | async-start | bytes 5242880 | tf_op jit(solution)/shard_map/all_gather | solution.py:106
  43.0 120.7 %all-gather.6.cloned.1.call-start = ((), (), s32[]{:S(2)}) async-start(), calls=%async_computation.4 | async-start | bytes 5242880 | tf_op jit(solution)/shard_map/all_gather | solution.py:106
  43.1 61.5 %copy-start.2 = (s32[160,1]{0,1:T(1,128)S(1)}, s32[160,1]{0,1:T(1,128)}, u32[]{:S(2)}) copy-start(s32[160,1]{0,1:T(1,128)} %param.5) | copy-start | bytes 1924
  72.1 59.4 %copy-start = (bf16[1,32,512]{2,1,0:T(8,128)(2,1)S(1)}, bf16[1,32,512]{2,1,0:T(8,128)(2,1)}, u32[]{:S(2)}) copy-start(bf16[1,32,512]{2,1,0:T(8,128)(2,1)} %param.7) | copy-start | bytes 98308
  72.1 91.7 %all-gather.10.cloned.1.call-start = ((), (), s32[]{:S(2)}) async-start(), calls=%async_computation.6 | async-start | bytes 5242880 | tf_op jit(solution)/shard_map/all_gather | solution.py:106
  100.9 29.1 %all-to-all-start.3 = ((bf16[8,128,512]{2,1,0:T(8,128)(2,1)}), bf16[8,128,512]{2,1,0:T(8,128)(2,1)S(1)}, u32[]{:S(2)}, u32[]{:S(2)}) async-start(bf16[8,128,512]{2,1,0:T(8,128)(2,1)} %get-tuple-element.5), calls=%async_computation.3 | async-start | bytes 2097152 | tf_op jit(solution)/shard_map/all_to_all | solution.py:103
  104.5 80.3 %all-gather.12.cloned.1.call-start = ((), (), s32[]{:S(2)}) async-start(), calls=%async_computation.7 | async-start | bytes 3276800 | tf_op jit(solution)/shard_map/all_gather | solution.py:106
  105.8 58.0 %copy-start.1 = (s32[20]{0:T(128)}, s32[20]{0:T(128)S(1)}, u32[]{:S(2)}) copy-start(s32[20]{0:T(128)S(1)} %get-tuple-element.9.owner_ref) | copy-start | bytes 244
Sparse Core Ops, SparseCore 0:
  43.2 33.4 all-gather.7
  78.3 34.4 all-gather.5
  114.3 34.4 all-gather.9
  150.3 25.5 all-gather.11

commit v2 on v0

v2 whole, which is shorter than its diff:
```python
import functools
import jax
import jax.numpy as jnp
from jax import lax
from jax.experimental import pallas as pl
from jax.experimental.pallas import tpu as pltpu
from jax.sharding import PartitionSpec as P

BLK = 512
DAMPING = 0.1
STRIDE = 5
LAG = 4
MESH = pl.DeviceIdType.MESH
VMEM_LIMIT = 60 * 1024 * 1024


def gather_kernel(
    owners, shards, per_peer,
    bases_ref, inverse_ref, full_ref, full_inverse_ref,
    own_sem, own_inverse_sem, move_send, move_recv, inverse_send, inverse_recv,
    row_send, row_recv, core_send, core_recv,
):
    me, shard = lax.axis_index("owner"), lax.axis_index("fsdp")
    chips = shards // 2
    chip, core = shard // 2, shard % 2
    sibling = chip * 2 + (1 - core)
    pieces = owners * per_peer

    def to(dst_shard, dst_owner):
        return (dst_shard, dst_owner)

    barrier = pltpu.get_barrier_semaphore()
    for step in range(1, owners):
        pl.semaphore_signal(barrier, inc=1, device_id=to(shard, (me + step) % owners), device_id_type=MESH)
    for step in range(1, chips):
        pl.semaphore_signal(barrier, inc=1, device_id=to((chip + step) % chips * 2 + core, me), device_id_type=MESH)
    pl.semaphore_signal(barrier, inc=1, device_id=to(sibling, me), device_id_type=MESH)
    pl.semaphore_wait(barrier, owners - 1 + chips)

    def place(index):
        return index // owners, index % owners

    def move(index):
        rank, turn = place(index)
        target = (me + turn * STRIDE) % owners
        return pltpu.make_async_remote_copy(
            src_ref=bases_ref.at[target, rank],
            dst_ref=full_ref.at[me, rank, shard],
            send_sem=move_send.at[index],
            recv_sem=move_recv.at[index],
            device_id=to(shard, target),
            device_id_type=MESH,
        )

    def move_inverse(turn):
        target = (me + turn * STRIDE) % owners
        return pltpu.make_async_remote_copy(
            src_ref=inverse_ref.at[target],
            dst_ref=full_inverse_ref.at[me],
            send_sem=inverse_send.at[turn],
            recv_sem=inverse_recv.at[turn],
            device_id=to(shard, target),
            device_id_type=MESH,
        )

    def piece(index, shard_of):
        rank, turn = place(index)
        source = (me + owners * STRIDE - turn * STRIDE) % owners
        return full_ref.at[source, rank, shard_of]

    def along_x(index, step):
        ref = piece(index, shard)
        return pltpu.make_async_remote_copy(
            src_ref=ref, dst_ref=ref,
            send_sem=row_send.at[step - 1, index],
            recv_sem=row_recv.at[step - 1, index],
            device_id=to((chip + step) % chips * 2 + core, me),
            device_id_type=MESH,
        )

    def across(index, step):
        ref = piece(index, (chip + chips - step) % chips * 2 + core)
        return pltpu.make_async_remote_copy(
            src_ref=ref, dst_ref=ref,
            send_sem=core_send.at[step, index],
            recv_sem=core_recv.at[step, index],
            device_id=to(sibling, me),
            device_id_type=MESH,
        )

    def own(rank):
        return pltpu.make_async_copy(bases_ref.at[me, rank], full_ref.at[me, rank, shard], own_sem.at[rank])

    own_inverse = pltpu.make_async_copy(inverse_ref.at[me], full_inverse_ref.at[me], own_inverse_sem)

    for rank in range(per_peer):
        own(rank).start()

    @pl.loop(0, pieces)
    def _(index):
        @pl.when(index % owners > 0)
        def _():
            move(index).start()

    own_inverse.start()

    @pl.loop(1, owners)
    def _(turn):
        move_inverse(turn).start()

    for rank in range(per_peer):
        own(rank).wait()

    def pass_on(index):
        for step in range(1, chips):
            along_x(index, step).wait_recv()
            across(index, step).start()

    @pl.loop(0, pieces)
    def _(index):
        @pl.when(index % owners > 0)
        def _():
            move(index).wait_recv()

        for step in range(1, chips):
            along_x(index, step).start()
        across(index, 0).start()

        @pl.when(index >= LAG)
        def _():
            pass_on(index - LAG)

    @pl.loop(pieces - LAG, pieces)
    def _(index):
        pass_on(index)

    own_inverse.wait()

    @pl.loop(1, owners)
    def _(turn):
        move_inverse(turn).wait()

    @pl.loop(0, pieces)
    def _(index):
        @pl.when(index % owners > 0)
        def _():
            move(index).wait_send()

        for step in range(1, chips):
            along_x(index, step).wait_send()
        for step in range(chips):
            across(index, step).wait()


def gather(bases, inverse):
    owners, shards = lax.axis_size("owner"), lax.axis_size("fsdp")
    per_peer = bases.shape[1]
    pieces, chips = owners * per_peer, shards // 2
    dma = pltpu.SemaphoreType.DMA
    anywhere = pl.BlockSpec(memory_space=pl.ANY)
    return pl.pallas_call(
        functools.partial(gather_kernel, owners, shards, per_peer),
        out_shape=(
            jax.ShapeDtypeStruct(bases.shape[:2] + (shards,) + bases.shape[2:], bases.dtype),
            jax.ShapeDtypeStruct(inverse.shape, inverse.dtype),
        ),
        in_specs=[anywhere, anywhere],
        out_specs=(anywhere, anywhere),
        scratch_shapes=[
            dma((per_peer,)), dma,
            dma((pieces,)), dma((pieces,)),
            dma((owners,)), dma((owners,)),
            dma((chips - 1, pieces)), dma((chips - 1, pieces)),
            dma((chips, pieces)), dma((chips, pieces)),
        ],
        compiler_params=pltpu.CompilerParams(
            collective_id=0, has_side_effects=True, vmem_limit_bytes=VMEM_LIMIT
        ),
        name="gather",
    )(bases, inverse)


def rotate_kernel(group, slot_ref, panel_ref, *refs):
    inverse_refs, basis_refs, out_ref = refs[:group], refs[group : 2 * group], refs[-1]
    for at in range(group):
        columns = slice(at * BLK, (at + 1) * BLK)
        basis = basis_refs[at][0]
        turned = jnp.dot(panel_ref[0, :, columns], basis, preferred_element_type=jnp.float32)
        scaled = (turned * inverse_refs[at][0]).astype(jnp.bfloat16)
        out_ref[0, :, columns] = lax.dot_general(
            scaled, basis, (((1,), (1,)), ((), ())), preferred_element_type=jnp.float32
        ).astype(jnp.bfloat16)


def rotate(slots, grads, inverse, bases):
    matrices, row_count, col_count = grads.shape
    block_count = col_count // BLK
    group = 2 if block_count % 2 == 0 else 1
    steps = block_count // group

    def panel_map(i, slot):
        return i // steps, 0, i % steps

    def slot_map(at, i, slot):
        return slot[i * group + at], 0, 0

    panel = pl.BlockSpec((1, row_count, group * BLK), panel_map)
    return pl.pallas_call(
        functools.partial(rotate_kernel, group),
        grid_spec=pltpu.PrefetchScalarGridSpec(
            num_scalar_prefetch=1,
            grid=(matrices * steps,),
            in_specs=[panel]
            + [pl.BlockSpec((1, 1, BLK), functools.partial(slot_map, at)) for at in range(group)]
            + [pl.BlockSpec((1, BLK, BLK), functools.partial(slot_map, at)) for at in range(group)],
            out_specs=panel,
        ),
        out_shape=jax.ShapeDtypeStruct(grads.shape, grads.dtype),
        compiler_params=pltpu.CompilerParams(vmem_limit_bytes=VMEM_LIMIT),
        cost_estimate=pl.CostEstimate(
            flops=4 * matrices * row_count * col_count * BLK,
            bytes_accessed=4 * matrices * row_count * col_count + 2 * matrices * col_count * BLK,
            transcendentals=0,
        ),
        name="rotate",
    )(slots, grads, *[inverse] * group, *[bases] * group)


def per_device(grads, assign, bases, eigvals):
    owner_count = lax.axis_size("owner")
    owner_here = lax.axis_index("owner")
    matrices, _, col_count = grads.shape
    unit_count = matrices * col_count // BLK
    slot_count = bases.shape[1]
    per_peer = slot_count // owner_count

    units = jnp.arange(unit_count, dtype=jnp.int32)
    owners = lax.dynamic_slice_in_dim(assign[:, 0], owner_here * unit_count, unit_count)
    earlier = units[None, :] < units[:, None]
    ranks = jnp.sum((owners[None, :] == owners[:, None]) & earlier, axis=1, dtype=jnp.int32)
    slots = owners * per_peer + ranks

    inverse = 1.0 / (eigvals[0].astype(jnp.float32) + DAMPING)
    full, full_inverse = gather(
        bases[0].reshape((owner_count, per_peer) + bases.shape[2:]),
        inverse.reshape(owner_count, per_peer, 1, BLK),
    )
    return rotate(
        slots, grads, full_inverse.reshape(slot_count, 1, BLK), full.reshape(slot_count, BLK, BLK)
    )


def solution(mesh):
    in_specs = (
        P("owner", "fsdp", None),
        P(),
        P("owner", None, "fsdp", None),
        P("owner", None, None),
    )
    out_specs = P("owner", "fsdp", None)
    return jax.shard_map(
        per_device, mesh=mesh, in_specs=in_specs, out_specs=out_specs, check_vma=False
    )
```

time: 272 us -> 156 us (0.57)
  Pallas kernels: 0 us -> 151 us
  blocking collectives: 101 us -> 0 us
  waiting for transfers between devices: 78 us -> 0 us
  local copies, waits for them, and re-layouts: 50.3 us -> 1.45 us
  matrix products: 23.2 us -> 0 us
  between operations: 13.4 us -> 0.01 us
  starting transfers between devices: 3.59 us -> 0 us
    pallas_call x0 -> x2, Pallas kernels: none -> 151 us  [the longest x1 130 us: gather(): pl.pallas_call(functools.partial(gather_kernel, owners, shards, per_peer)...]
    all_to_all x1 -> x0, blocking collectives: 101 us -> none  [per_device(): lax.all_to_all(base_local, 'owner', split_axis=0, concat_axis=0, tiled=True)]
    all_gather x1 -> x0, waiting for transfers between devices: 78 us -> none  [per_device(): full_bases = lax.all_gather(moved_bases, 'fsdp', axis=1, tiled=True)]
    dot_general x1 -> x0, matrix products: 23.2 us -> none  [rotate(): jnp.einsum('srk,sck->src', scaled, basis_block, preferred_element_type=jn...]
    unnamed x2 -> x0, local copies, waits for them, and re-layouts: 19.3 us -> none
    reshape x1 -> x0, local copies, waits for them, and re-layouts: 17.6 us -> none  [per_device(): return finished.reshape(matrices, block_count, row_count, BLK).transpose(...]
    gather x2 -> x0, local copies, waits for them, and re-layouts: 11.9 us -> none  [per_device(): finished = rotate(panels, full_bases[my_slots], moved_eigen[my_slots])]
    all_to_all x1 -> x0, starting transfers between devices: 3.59 us -> none  [per_device(): lax.all_to_all(eigen_local, 'owner', split_axis=0, concat_axis=0, tiled=T...]
  transfers between devices with their start and end apart: 2 -> 0, of which waited for: 1 -> 0; matrix products, arithmetic and copies ran while one was open for 8% -> 0% of each run, Pallas kernels for 0% -> 0%
where the time goes in v2:
time: 156 us; the launch traced here: 155 us
  Pallas kernels  151 us (97%)
  other arithmetic  2.23 us (1%)
    pallas_call x1, Pallas kernels, gather(): pl.pallas_call(functools.partial(gather_kernel, owners, shards, per_peer)...  130 us
    pallas_call x1, Pallas kernels, rotate(): pl.pallas_call(functools.partial(rotate_kernel, group), grid_spec=pltpu.P...  21.4 us

profile of v2, /device:TPU:0, one launch (start us, length us, event | category | flops | bytes accessed | tf_op | source)
XLA Modules:
  0.0 155.0 jit_solution(17689330804439344708)
XLA Ops:
  0.0 0.8 dynamic-slice_bitcast_fusion
  0.8 0.2 convert_reduce_fusion
  0.9 1.3 multiply_add_fusion.slot_ref
  2.2 0.8 add_divide_fusion
  3.0 0.7 div.18.inverse_ref
  3.7 130.0 %gather.1 = (bf16[8,4,4,128,512]{4,3,2,1,0:T(8,128)(2,1)}, f32[8,4,1,512]{3,2,1,0:T(1,128)}) custom-call(bf16[8,4,128,512]{3,2,1,0:T(8,128)(2,1)} %bitcast.9, f32[8,4,1,512]{3,2,1,0:T(1,128)} %div.18.inverse_ref), custom_call_target="tpu_custom_call" | custom-call | tf_op jit(solution)/shard_map/gather/pallas_call | solution.py:161
  133.7 21.4 %rotate.1 = bf16[2,640,5120]{2,1,0:T(8,128)(2,1)} custom-call(s32[20]{0:T(128)} %multiply_add_fusion.slot_ref, bf16[2,640,5120]{2,1,0:T(8,128)(2,1)} %panel_ref.1, f32[32,1,512]{2,1,0:T(1,128)} %bitcast.10, f32[32,1,512]{2,1,0:T(1,128)} %bitcast.11, bf16[32,512,512]{2,1,0:T(8,128)(2,1)} %bitcast.7, bf16[32,512,512]{2,1,0:T(8,128)(2,1)} %bitcast.8), custom_call_target="tpu_custom_call" | custom-call | flops 13421772800 | bytes 36700160 | tf_op jit(solution)/shard_map/rotate/pallas_call | solution.py:208

commit v3 on v2

--- a/solution.py
+++ b/solution.py
@@ -8,8 +8,8 @@
 
 BLK = 512
 DAMPING = 0.1
-STRIDE = 5
 LAG = 4
+WINDOW = 6
 MESH = pl.DeviceIdType.MESH
 VMEM_LIMIT = 60 * 1024 * 1024
 
@@ -40,9 +40,17 @@
     def place(index):
         return index // owners, index % owners
 
+    def partner(turn):
+        across_bits = turn % 2 * (owners // 2) + turn // 2
+        other, bit = 0, 1
+        while bit < owners:
+            other = other + (me // bit % 2 + across_bits // bit % 2) % 2 * bit
+            bit *= 2
+        return other
+
     def move(index):
         rank, turn = place(index)
-        target = (me + turn * STRIDE) % owners
+        target = partner(turn)
         return pltpu.make_async_remote_copy(
             src_ref=bases_ref.at[target, rank],
             dst_ref=full_ref.at[me, rank, shard],
@@ -53,7 +61,7 @@
         )
 
     def move_inverse(turn):
-        target = (me + turn * STRIDE) % owners
+        target = partner(turn)
         return pltpu.make_async_remote_copy(
             src_ref=inverse_ref.at[target],
             dst_ref=full_inverse_ref.at[me],
@@ -65,8 +73,7 @@
 
     def piece(index, shard_of):
         rank, turn = place(index)
-        source = (me + owners * STRIDE - turn * STRIDE) % owners
-        return full_ref.at[source, rank, shard_of]
+        return full_ref.at[partner(turn), rank, shard_of]
 
     def along_x(index, step):
         ref = piece(index, shard)
@@ -96,11 +103,9 @@
     for rank in range(per_peer):
         own(rank).start()
 
-    @pl.loop(0, pieces)
-    def _(index):
-        @pl.when(index % owners > 0)
-        def _():
-            move(index).start()
+    @pl.loop(1, 1 + WINDOW)
+    def _(index):
+        move(index).start()
 
     own_inverse.start()
 
@@ -125,6 +130,11 @@
         for step in range(1, chips):
             along_x(index, step).start()
         across(index, 0).start()
+        later = index + 1 + WINDOW
+
+        @pl.when((later < pieces) & (later % owners > 0))
+        def _():
+            move(later).start()
 
         @pl.when(index >= LAG)
         def _():
@@ -182,13 +192,14 @@
 
 def rotate_kernel(group, slot_ref, panel_ref, *refs):
     inverse_refs, basis_refs, out_ref = refs[:group], refs[group : 2 * group], refs[-1]
+    scaled = []
     for at in range(group):
-        columns = slice(at * BLK, (at + 1) * BLK)
-        basis = basis_refs[at][0]
-        turned = jnp.dot(panel_ref[0, :, columns], basis, preferred_element_type=jnp.float32)
-        scaled = (turned * inverse_refs[at][0]).astype(jnp.bfloat16)
-        out_ref[0, :, columns] = lax.dot_general(
-            scaled, basis, (((1,), (1,)), ((), ())), preferred_element_type=jnp.float32
+        panel = panel_ref[0, :, at * BLK : (at + 1) * BLK]
+        turned = jnp.dot(panel, basis_refs[at][0], preferred_element_type=jnp.float32)
+        scaled.append((turned * inverse_refs[at][0]).astype(jnp.bfloat16))
+    for at in range(group):
+        out_ref[0, :, at * BLK : (at + 1) * BLK] = lax.dot_general(
+            scaled[at], basis_refs[at][0], (((1,), (1,)), ((), ())), preferred_element_type=jnp.float32
         ).astype(jnp.bfloat16)
 
 

time: 156 us -> 144 us (0.923)
  Pallas kernels: 151 us -> 140 us
    pallas_call x1, Pallas kernels: 130 us -> 119 us  [gather(): pl.pallas_call(functools.partial(gather_kernel, owners, shards, per_peer)...]
where the time goes in v3:
time: 144 us
  Pallas kernels  140 us (97%)
  other arithmetic  2.23 us (2%)
  local copies, waits for them, and re-layouts  1.45 us (1%)
    pallas_call x1, Pallas kernels, gather(): pl.pallas_call(functools.partial(gather_kernel, owners, shards, per_peer)...  119 us
    pallas_call x1, Pallas kernels, rotate(): pl.pallas_call(functools.partial(rotate_kernel, group), grid_spec=pltpu.P...  21.4 us

profile of v3, /device:TPU:0, one launch (start us, length us, event | category | flops | bytes accessed | tf_op | source)
XLA Modules:
  0.0 143.9 jit_solution(5797255525111207404)
XLA Ops:
  0.0 0.8 dynamic-slice_bitcast_fusion
  0.8 0.2 convert_reduce_fusion
  0.9 1.3 multiply_add_fusion.slot_ref
  2.2 0.8 add_divide_fusion
  3.0 0.7 div.18.inverse_ref
  3.7 118.8 %gather.1 = (bf16[8,4,4,128,512]{4,3,2,1,0:T(8,128)(2,1)}, f32[8,4,1,512]{3,2,1,0:T(1,128)}) custom-call(bf16[8,4,128,512]{3,2,1,0:T(8,128)(2,1)} %bitcast.9, f32[8,4,1,512]{3,2,1,0:T(1,128)} %div.18.inverse_ref), custom_call_target="tpu_custom_call" | custom-call | tf_op jit(solution)/shard_map/gather/pallas_call | solution.py:171
  122.5 21.4 %rotate.1 = bf16[2,640,5120]{2,1,0:T(8,128)(2,1)} custom-call(s32[20]{0:T(128)} %multiply_add_fusion.slot_ref, bf16[2,640,5120]{2,1,0:T(8,128)(2,1)} %panel_ref.1, f32[32,1,512]{2,1,0:T(1,128)} %bitcast.10, f32[32,1,512]{2,1,0:T(1,128)} %bitcast.11, bf16[32,512,512]{2,1,0:T(8,128)(2,1)} %bitcast.7, bf16[32,512,512]{2,1,0:T(8,128)(2,1)} %bitcast.8), custom_call_target="tpu_custom_call" | custom-call | flops 13421772800 | bytes 36700160 | tf_op jit(solution)/shard_map/rotate/pallas_call | solution.py:219

commit v4 on v3

--- a/solution.py
+++ b/solution.py
@@ -8,7 +8,7 @@
 
 BLK = 512
 DAMPING = 0.1
-LAG = 4
+LAG = 8
 WINDOW = 6
 MESH = pl.DeviceIdType.MESH
 VMEM_LIMIT = 60 * 1024 * 1024
@@ -206,7 +206,7 @@
 def rotate(slots, grads, inverse, bases):
     matrices, row_count, col_count = grads.shape
     block_count = col_count // BLK
-    group = 2 if block_count % 2 == 0 else 1
+    group = 5 if block_count % 5 == 0 else 1
     steps = block_count // group
 
     def panel_map(i, slot):

time: 144 us -> 143 us (level)
  no operation moved by 1% of the time
where the time goes in v4:
time: 143 us
  Pallas kernels  139 us (97%)
  other arithmetic  2.23 us (2%)
  local copies, waits for them, and re-layouts  1.45 us (1%)
    pallas_call x1, Pallas kernels, gather(): pl.pallas_call(functools.partial(gather_kernel, owners, shards, per_peer)...  119 us
    pallas_call x1, Pallas kernels, rotate(): pl.pallas_call(functools.partial(rotate_kernel, group), grid_spec=pltpu.P...  20.1 us

profile of v4, /device:TPU:0, one launch (start us, length us, event | category | flops | bytes accessed | tf_op | source)
XLA Modules:
  0.0 142.6 jit_solution(364526402097257016)
XLA Ops:
  0.0 0.8 dynamic-slice_bitcast_fusion
  0.8 0.2 convert_reduce_fusion
  0.9 1.3 multiply_add_fusion.slot_ref
  2.2 0.8 add_divide_fusion
  3.0 0.7 div.18.inverse_ref
  3.7 118.8 %gather.1 = (bf16[8,4,4,128,512]{4,3,2,1,0:T(8,128)(2,1)}, f32[8,4,1,512]{3,2,1,0:T(1,128)}) custom-call(bf16[8,4,128,512]{3,2,1,0:T(8,128)(2,1)} %bitcast.12, f32[8,4,1,512]{3,2,1,0:T(1,128)} %div.18.inverse_ref), custom_call_target="tpu_custom_call" | custom-call | tf_op jit(solution)/shard_map/gather/pallas_call | solution.py:171
  122.5 20.1 %rotate.1 = bf16[2,640,5120]{2,1,0:T(8,128)(2,1)} custom-call(s32[20]{0:T(128)} %multiply_add_fusion.slot_ref, bf16[2,640,5120]{2,1,0:T(8,128)(2,1)} %panel_ref.1, f32[32,1,512]{2,1,0:T(1,128)} %bitcast.13, f32[32,1,512]{2,1,0:T(1,128)} %bitcast.14, f32[32,1,512]{2,1,0:T(1,128)} %bitcast.15, f32[32,1,512]{2,1,0:T(1,128)} %bitcast.16, ...), custom_call_target="tpu_custom_call" | custom-call | flops 13421772800 | bytes 36700160 | tf_op jit(solution)/shard_map/rotate/pallas_call | solution.py:219
